TPU v7x, 128 devices: a whole 4x4x4 slice. The times are simulated.
128 devices in a mesh: lev: 4 (over y), col: 32 (over x, z, core).
Axes of the slice: x: 4, y: 4, z: 4, core: 2. Of those that a mesh axis runs over, the one named last changes fastest.
Arguments:
- increment: bfloat16 [3, 128, 131072], P(None, 'lev', 'col'), may hold values from -6 to 6
- jacobian: bfloat16 [1024, 616, 384], P(('lev', 'col')), may hold values from -0.3125 to 0.3125
- departure: bfloat16 [616, 1048576], P(None, ('lev', 'col')), may hold values from -6 to 6
- predictor: float32 [8, 1048576], P(None, ('lev', 'col')), may hold values from -5 to 5
- bias_coef: float32 [616, 8], replicated, may hold values from -1.5 to 1.5
- obs_sigma: float32 [616], replicated, may hold values from 0.5 to 2
- channel_use: int32 [1024, 616], P(('lev', 'col')), may hold values 0 or 1
- send_cols: int32 [128, 128, 8], P(('lev', 'col')), may hold values from 0 to 1023
- obs_slot: int32 [1048576], P(('lev', 'col')), may hold values from 0 to 1023, as said below
Outputs:
- gradient: float32 [3, 128, 131072], P(None, 'lev', 'col')
Inputs may be any that keep to these rules, and one draw needn't show every extreme that they name: obs_slot[j] = s * 8 + k; the slots (s, p, k) named by the observations of device p are, for each s, the first few of the 8, at least 2 of them; some device p names all 8 slots of every device.
All inputs are finite; a program needn't handle non-finite values. No bound on the sum of `channel_use` on one device may be relied on, other than what follows from the above.
Results may differ from a plain program's by a relative error of at most 0.001.
Values may be sent and summed in bfloat16 or wider, within the bound.
A program may use at most 128 MiB of HBM per device.

v0:
```python
import jax
import jax.numpy as jnp
from jax import lax
from jax.sharding import PartitionSpec as P


def fetch_rows(outgoing):
    return lax.all_to_all(outgoing, ("lev", "col"), split_axis=0, concat_axis=0, tiled=True)


def return_rows(outgoing):
    return lax.all_to_all(outgoing, ("lev", "col"), split_axis=0, concat_axis=0, tiled=True)


def observe(profile, jacobian, departure, predictor, bias_coef, obs_sigma, channel_use):
    tile_count = jacobian.shape[0]
    channels = jacobian.shape[1]
    obs_count = profile.shape[0]
    profile_len = profile.shape[1]
    obs_tile = obs_count // tile_count
    tangent = jnp.einsum(
        "tcf,tof->cto",
        jacobian,
        profile.reshape(tile_count, obs_tile, profile_len),
        preferred_element_type=jnp.float32,
    )
    bias_term = jnp.dot(
        bias_coef, predictor, precision=lax.Precision.HIGHEST, preferred_element_type=jnp.float32
    )
    residual = tangent - (departure.astype(jnp.float32) - bias_term).reshape(
        channels, tile_count, obs_tile
    )
    inverse_var = 1.0 / (obs_sigma * obs_sigma)
    scaling = channel_use.astype(jnp.float32).T * inverse_var[:, None]
    forcing = (scaling[:, :, None] * residual).astype(jnp.bfloat16)
    return jnp.einsum(
        "tcf,cto->tof", jacobian, forcing, preferred_element_type=jnp.float32
    ).reshape(obs_count, profile_len)


def on_device(
    increment,
    jacobian,
    departure,
    predictor,
    bias_coef,
    obs_sigma,
    channel_use,
    send_cols,
    obs_slot,
):
    lev_size = lax.axis_size("lev")
    col_size = lax.axis_size("col")
    peer_count = lev_size * col_size
    field_count = increment.shape[0]
    capacity = send_cols.shape[2]
    columns = lax.all_to_all(increment, "lev", split_axis=2, concat_axis=1, tiled=True)
    level_count = columns.shape[1]
    column_count = columns.shape[2]
    profile_len = field_count * level_count
    column_rows = columns.reshape(profile_len, column_count).T
    slot_lists = send_cols[0]
    outgoing = column_rows[slot_lists]
    incoming = fetch_rows(outgoing).reshape(peer_count * capacity, profile_len)
    profile = incoming[obs_slot]
    adjoint = observe(profile, jacobian, departure, predictor, bias_coef, obs_sigma, channel_use)
    slot_adjoint = jax.ops.segment_sum(adjoint, obs_slot, num_segments=peer_count * capacity)
    returned = return_rows(slot_adjoint.reshape(peer_count, capacity, profile_len))
    column_adjoint = jax.ops.segment_sum(
        returned.reshape(peer_count * capacity, profile_len),
        slot_lists.reshape(-1),
        num_segments=column_count,
    )
    field_adjoint = column_adjoint.T.reshape(field_count, level_count, column_count)
    return lax.all_to_all(field_adjoint, "lev", split_axis=1, concat_axis=2, tiled=True)


def solution(mesh):
    return jax.shard_map(
        on_device,
        mesh=mesh,
        in_specs=(
            P(None, "lev", "col"),
            P(("lev", "col"), None, None),
            P(None, ("lev", "col")),
            P(None, ("lev", "col")),
            P(),
            P(),
            P(("lev", "col"), None),
            P(("lev", "col"), None, None),
            P(("lev", "col")),
        ),
        out_specs=P(None, "lev", "col"),
        check_vma=False,
    )
```

profile of v0, /device:TPU:0, one launch (start us, length us, event | category | flops | bytes accessed | tf_op | source)
XLA Modules:
  0.0 255.4 jit_solution(5134098283058532032)
XLA Ops:
  0.0 0.0 copy-start
  0.0 6.0 %copy.31 = bf16[3,32,4096]{1,0,2:T(4,128)(2,1)} copy(bf16[3,32,4096]{2,1,0:T(8,128)(2,1)} %param.9) | data formatting | bytes 1572864 | tf_op args[0]
  6.0 5.6 %reshape.103 = bf16[4,2,49152]{2,1,0:T(2,128)(2,1)} reshape(bf16[4096,3,32]{2,1,0:T(4,128)(2,1)} %bitcast.49) | data formatting | bytes 1572864
  11.6 4.5 %all-to-all-start = ((bf16[4,2,49152]{2,1,0:T(2,128)(2,1)}), bf16[4,2,49152]{2,1,0:T(2,128)(2,1)S(1)}, u32[]{:S(2)}, u32[]{:S(2)}) async-start(bf16[4,2,49152]{2,1,0:T(2,128)(2,1)} %reshape.103), calls=%async_computation | async-start | bytes 1572864 | tf_op jit(solution)/shard_map/all_to_all | solution.py:57
  16.2 0.0 copy-done.5
  16.2 0.1 copy.35
  16.3 0.1 reshape.65
  16.4 0.0 copy-done.6
  16.5 12.0 %all-to-all-done = bf16[4,2,49152]{2,1,0:T(2,128)(2,1)S(1)} async-done(((bf16[4,2,49152]{2,1,0:T(2,128)(2,1)}), bf16[4,2,49152]{2,1,0:T(2,128)(2,1)S(1)}, u32[]{:S(2)}, u32[]{:S(2)}) %all-to-all-start) | async-done | bytes 786464 | tf_op jit(solution)/shard_map/all_to_all | solution.py:57
  28.5 4.2 %reshape.104 = bf16[4096,3,32]{2,1,0:T(4,128)(2,1)} reshape(bf16[4,2,49152]{2,1,0:T(2,128)(2,1)S(1)} %all-to-all-done) | data formatting | bytes 1572864
  32.6 5.3 %copy.33 = bf16[3,4,32,1024]{3,2,1,0:T(8,128)(2,1)S(1)} copy(bf16[3,4,32,1024]{2,0,3,1:T(4,128)(2,1)} %bitcast.48) | data formatting | bytes 1572864 | tf_op jit(solution)/shard_map/all_to_all | solution.py:57
  38.0 0.4 copy.34
  38.3 0.0 copy-start.3
  38.4 5.0 %gather_fusion = bf16[1024,384]{1,0:T(8,128)(2,1)} fusion(bf16[1024,384]{1,0:T(8,128)(2,1)S(1)} %bitcast.46, s32[1024]{0:T(1024)S(1)} %broadcast_clamp_fusion), kind=kCustom, calls=%fused_computation | custom fusion | bytes 1576960 | tf_op jit(solution)/shard_map/gather | solution.py:63
  43.4 9.2 %all-to-all-start.1 = ((bf16[128,8,384]{2,1,0:T(8,128)(2,1)}), bf16[128,8,384]{2,1,0:T(8,128)(2,1)S(1)}, u32[]{:S(2)}, u32[]{:S(2)}) async-start(bf16[128,8,384]{2,1,0:T(8,128)(2,1)} %bitcast.7), calls=%async_computation.1 | async-start | bytes 1572864 | tf_op jit(solution)/shard_map/all_to_all | solution.py:8
  52.6 20.8 %convert_subtract_fusion = f32[616,8192]{1,0:T(8,128)} fusion(bf16[616,8192]{1,0:T(8,128)(2,1)} %param.11, f32[616,8]{0,1:T(8,128)S(1)} %copy-done.3, f32[8,8192]{1,0:T(8,128)S(1)} %copy-done), kind=kOutput, calls=%fused_computation.7 | convolution fusion | flops 494534656 | bytes 30559488 | tf_op jit(solution)/shard_map/dot_general | solution.py:27
  73.4 0.0 all-to-all-done.1
  73.4 33.1 %gather_fusion.1 = bf16[8192,384]{1,0:T(8,128)(2,1)} fusion(bf16[1024,384]{1,0:T(8,128)(2,1)S(1)} %bitcast.45, s32[8192]{0:T(1024)S(1)} %fusion.12), kind=kCustom, calls=%fused_computation.1 | custom fusion | bytes 12615680 | tf_op jit(solution)/shard_map/gather | solution.py:65
  106.5 24.5 %fusion.2 = f32[8,1024,384]{2,1,0:T(8,128)} fusion(bf16[8,616,384]{2,1,0:T(8,128)(2,1)} %param.10, f32[77,8,8,1024]{3,2,1,0:T(8,128)} %bitcast.47, f32[616,8]{0,1:T(8,128)S(1)} %multiply_bitcast_fusion, bf16[8,1024,384]{2,1,0:T(8,128)(2,1)} %bitcast.50), kind=kOutput, calls=%fused_computation.8 | convolution fusion | flops 7766212608 | bytes 42863872 | tf_op jit(solution)/shard_map/tcf,cto->tof/dot_general | solution.py:36
  131.0 50.4 %scatter_custom_fusion = f32[1024,384]{1,0:T(8,128)} fusion(s32[8192]{0:T(1024)S(1)} %copy-done.2, f32[8192,384]{1,0:T(8,128)} %bitcast.55, f32[]{:T(128)} %constant.4.clone.1), kind=kCustom, calls=%fused_computation.14 | custom fusion | flops 3145728 | bytes 1573376 | tf_op jit(solution)/shard_map/scatter-add | solution.py:67
  181.5 9.6 %all-to-all-start.2 = ((f32[128,8,384]{2,1,0:T(8,128)}), f32[128,8,384]{2,1,0:T(8,128)S(1)}, u32[]{:S(2)}, u32[]{:S(2)}) async-start(f32[128,8,384]{2,1,0:T(8,128)} %bitcast.12), calls=%async_computation.2 | async-start | bytes 3145728 | tf_op jit(solution)/shard_map/all_to_all | solution.py:12
  191.0 0.1 copy.30
  191.1 0.1 reshape.89
  191.2 24.7 %all-to-all-done.2 = f32[128,8,384]{2,1,0:T(8,128)S(1)} async-done(((f32[128,8,384]{2,1,0:T(8,128)}), f32[128,8,384]{2,1,0:T(8,128)S(1)}, u32[]{:S(2)}, u32[]{:S(2)}) %all-to-all-start.2) | async-done | bytes 1572896 | tf_op jit(solution)/shard_map/all_to_all | solution.py:12
  215.9 7.1 %scatter_custom_fusion.1 = f32[1024,384]{1,0:T(8,128)S(1)} fusion(s32[1024]{0:T(1024)S(1)} %reshape.89, f32[128,8,384]{2,1,0:T(8,128)S(1)} %all-to-all-done.2, f32[]{:T(128)} %constant.4.clone.1), kind=kCustom, calls=%fused_computation.11 | custom fusion | flops 393216 | bytes 3145732 | tf_op jit(solution)/shard_map/scatter-add | solution.py:69
  223.0 0.5 copy.37
  223.5 1.1 copy.38
  224.5 0.0 copy-start.1
  224.6 28.6 %all_to_all.43 = f32[3,128,1024]{2,0,1:T(4,128)S(1)} all-to-all(f32[3,128,1024]{2,0,1:T(4,128)S(1)} %copy.38), channel_id=1, replica_groups=mesh['lev'=4,'col'=32] {'lev'}, dimensions={1} | all-to-all | bytes 3145728 | tf_op jit(solution)/shard_map/all_to_all | solution.py:75
  253.2 0.9 copy.39
  254.1 1.3 copy.44
  255.4 0.0 copy-done.1
  (13 shorter events, 0.0 us)
Async XLA Ops:
  0.0 52.6 %copy-start = (f32[8,8192]{1,0:T(8,128)S(1)}, f32[8,8192]{1,0:T(8,128)}, u32[]{:S(2)}) copy-start(f32[8,8192]{1,0:T(8,128)} %param.12) | copy-start | bytes 786436
  6.0 10.1 %copy-start.5 = (s32[1,128,8]{1,2,0:T(8,128)S(1)}, s32[1,128,8]{1,2,0:T(8,128)}, u32[]{:S(2)}) copy-start(s32[1,128,8]{1,2,0:T(8,128)} %param.16) | copy-start | bytes 12292
  6.0 10.4 %copy-start.6 = (f32[616]{0:T(1024)S(1)}, f32[616]{0:T(1024)}, u32[]{:S(2)}) copy-start(f32[616]{0:T(1024)} %param.14) | copy-start | bytes 7396
  6.0 10.4 %copy-start.4 = (s32[8,616]{1,0:T(8,128)S(1)}, s32[8,616]{1,0:T(8,128)}, u32[]{:S(2)}) copy-start(s32[8,616]{1,0:T(8,128)} %param.15) | copy-start | bytes 59140
  6.0 10.4 %copy-start.2 = (s32[8192]{0:T(1024)S(1)}, s32[8192]{0:T(1024)}, u32[]{:S(2)}) copy-start(s32[8192]{0:T(1024)} %param.17) | copy-start | bytes 98308
  11.6 16.8 %all-to-all-start = ((bf16[4,2,49152]{2,1,0:T(2,128)(2,1)}), bf16[4,2,49152]{2,1,0:T(2,128)(2,1)S(1)}, u32[]{:S(2)}, u32[]{:S(2)}) async-start(bf16[4,2,49152]{2,1,0:T(2,128)(2,1)} %reshape.103), calls=%async_computation | async-start | bytes 1572864 | tf_op jit(solution)/shard_map/all_to_all | solution.py:57
  38.3 14.2 %copy-start.3 = (f32[616,8]{0,1:T(8,128)S(1)}, f32[616,8]{0,1:T(8,128)}, u32[]{:S(2)}) copy-start(f32[616,8]{0,1:T(8,128)} %param.13) | copy-start | bytes 59140
  43.4 30.0 %all-to-all-start.1 = ((bf16[128,8,384]{2,1,0:T(8,128)(2,1)}), bf16[128,8,384]{2,1,0:T(8,128)(2,1)S(1)}, u32[]{:S(2)}, u32[]{:S(2)}) async-start(bf16[128,8,384]{2,1,0:T(8,128)(2,1)} %bitcast.7), calls=%async_computation.1 | async-start | bytes 1572864 | tf_op jit(solution)/shard_map/all_to_all | solution.py:8
  181.5 34.5 %all-to-all-start.2 = ((f32[128,8,384]{2,1,0:T(8,128)}), f32[128,8,384]{2,1,0:T(8,128)S(1)}, u32[]{:S(2)}, u32[]{:S(2)}) async-start(f32[128,8,384]{2,1,0:T(8,128)} %bitcast.12), calls=%async_computation.2 | async-start | bytes 3145728 | tf_op jit(solution)/shard_map/all_to_all | solution.py:12
  224.5 30.9 %copy-start.1 = (f32[8,8192]{1,0:T(8,128)S(1)}, f32[8,8192]{1,0:T(8,128)}, u32[]{:S(2)}) copy-start(f32[8,8192]{1,0:T(8,128)} %param.12) | copy-start | bytes 786436
where the time goes:
time: 256 us; the launch traced here: 255 us
  local copies, waits for them, and re-layouts  63.8 us (25%)
  other arithmetic  57.5 us (22%)
  matrix products  45.3 us (18%)
  waiting for transfers between devices  36.7 us (14%)
  blocking collectives  28.6 us (11%)
  starting transfers between devices  23.3 us (9%)
    scatter-add x1, other arithmetic, on_device(): jax.ops.segment_sum(adjoint, obs_slot, num_segments=peer_count * capacity)  50.4 us
    gather x1, local copies, waits for them, and re-layouts, on_device(): profile = incoming[obs_slot]  33.1 us
    all_to_all x1, blocking collectives, on_device(): lax.all_to_all(field_adjoint, 'lev', split_axis=1, concat_axis=2, tiled=T...  28.6 us
    all_to_all x1, waiting for transfers between devices, return_rows(): lax.all_to_all(outgoing, ('lev', 'col'), split_axis=0, concat_axis=0, til...  24.7 us
    dot_general x1, matrix products, observe(): jnp.einsum('tcf,cto->tof', jacobian, forcing, preferred_element_type=jnp....  24.5 us
    dot_general x1, matrix products, observe(): jnp.dot(bias_coef, predictor, precision=lax.Precision.HIGHEST, preferred_...  20.8 us
    unnamed x18, local copies, waits for them, and re-layouts  15.9 us
    all_to_all x1, waiting for transfers between devices, on_device(): lax.all_to_all(increment, 'lev', split_axis=2, concat_axis=1, tiled=True)  12 us
  transfers between devices with their start and end apart: 3, of which 2 were waited for; matrix products, arithmetic and copies ran while one was open for 8% of the time, Pallas kernels for 0%

commit v1 on v0

--- a/solution.py
+++ b/solution.py
@@ -2,6 +2,29 @@
 import jax.numpy as jnp
 from jax import lax
 from jax.sharding import PartitionSpec as P
+
+
+def in_blocks(x, dim, size):
+    before, after = (x.shape[:dim], x.shape[dim + 1 :])
+    return jnp.moveaxis(x.reshape(*before, size, -1, *after), dim, 0)
+
+
+def joined_along(blocks, dim):
+    blocks = jnp.moveaxis(blocks, 0, dim)
+    lengths = blocks.shape
+    return blocks.reshape(*lengths[:dim], lengths[dim] * lengths[dim + 1], *lengths[dim + 2 :])
+
+
+def rotated_exchange(x, axis, split_dim, concat_dim):
+    size, position = (lax.axis_size(axis), lax.axis_index(axis))
+    blocks = in_blocks(x, split_dim, size)
+    out = blocks
+    for turn in range(1, size):
+        target, source = ((position + turn) % size, (position - turn) % size)
+        sent = lax.dynamic_index_in_dim(blocks, target, 0)
+        other = lax.ppermute(sent, axis, [(i, (i + turn) % size) for i in range(size)])
+        out = lax.dynamic_update_slice_in_dim(out, other, source, axis=0)
+    return joined_along(out, concat_dim)
 
 
 def fetch_rows(outgoing):
@@ -54,7 +77,7 @@
     peer_count = lev_size * col_size
     field_count = increment.shape[0]
     capacity = send_cols.shape[2]
-    columns = lax.all_to_all(increment, "lev", split_axis=2, concat_axis=1, tiled=True)
+    columns = rotated_exchange(increment, "lev", 2, 1)
     level_count = columns.shape[1]
     column_count = columns.shape[2]
     profile_len = field_count * level_count

time: 256 us -> 251 us (0.980)
  local copies, waits for them, and re-layouts: 63.8 us -> 54.4 us
  starting transfers between devices: 23.3 us -> 27 us
    unnamed x18 -> x15, local copies, waits for them, and re-layouts: 15.9 us -> 0.13 us
    ppermute x0 -> x3, waiting for transfers between devices: none -> 13 us  [rotated_exchange(): lax.ppermute(sent, axis, [(i, (i + turn) % size) for i in range(size)])]
    all_to_all x1 -> x0, waiting for transfers between devices: 12 us -> none  [on_device(): lax.all_to_all(increment, 'lev', split_axis=2, concat_axis=1, tiled=True)]
    dynamic_update_slice x0 -> x3, local copies, waits for them, and re-layouts: none -> 7.9 us  [rotated_exchange(): out = lax.dynamic_update_slice_in_dim(out, other, source, axis=0)]
    ppermute x0 -> x3, starting transfers between devices: none -> 5.98 us  [rotated_exchange(): lax.ppermute(sent, axis, [(i, (i + turn) % size) for i in range(size)])]
    all_to_all x1 -> x0, local copies, waits for them, and re-layouts: 5.34 us -> none  [on_device(): lax.all_to_all(increment, 'lev', split_axis=2, concat_axis=1, tiled=True)]
    all_to_all x1 -> x0, starting transfers between devices: 4.55 us -> none  [on_device(): lax.all_to_all(increment, 'lev', split_axis=2, concat_axis=1, tiled=True)]
  transfers between devices with their start and end apart: 3 -> 5, of which waited for: 2 -> 3; matrix products, arithmetic and copies ran while one was open for 8% -> 11% of each run, Pallas kernels for 0% -> 0%
where the time goes in v1:
time: 251 us
  other arithmetic  57.5 us (23%)
  local copies, waits for them, and re-layouts  54.4 us (22%)
  matrix products  45.2 us (18%)
  waiting for transfers between devices  37.6 us (15%)
  blocking collectives  28.6 us (11%)
  starting transfers between devices  27 us (11%)
    scatter-add x1, other arithmetic, on_device(): jax.ops.segment_sum(adjoint, obs_slot, num_segments=peer_count * capacity)  50.4 us
    gather x1, local copies, waits for them, and re-layouts, on_device(): profile = incoming[obs_slot]  33.1 us
    all_to_all x1, blocking collectives, on_device(): lax.all_to_all(field_adjoint, 'lev', split_axis=1, concat_axis=2, tiled=T...  28.6 us
    all_to_all x1, waiting for transfers between devices, return_rows(): lax.all_to_all(outgoing, ('lev', 'col'), split_axis=0, concat_axis=0, til...  24.7 us
    dot_general x1, matrix products, observe(): jnp.einsum('tcf,cto->tof', jacobian, forcing, preferred_element_type=jnp....  24.5 us
    dot_general x1, matrix products, observe(): jnp.dot(bias_coef, predictor, precision=lax.Precision.HIGHEST, preferred_...  20.8 us
    ppermute x3, waiting for transfers between devices, rotated_exchange(): lax.ppermute(sent, axis, [(i, (i + turn) % size) for i in range(size)])  13 us
    all_to_all x1, starting transfers between devices, fetch_rows(): lax.all_to_all(outgoing, ('lev', 'col'), split_axis=0, concat_axis=0, til...  11.5 us
  transfers between devices with their start and end apart: 5, of which 3 were waited for; matrix products, arithmetic and copies ran while one was open for 11% of the time, Pallas kernels for 0%

profile of v1, /device:TPU:0, one launch (start us, length us, event | category | flops | bytes accessed | tf_op | source)
XLA Modules:
  0.0 250.8 jit_solution(10784754709084254040)
XLA Ops:
  0.1 2.3 reshape.57
  2.4 1.2 dynamic-slice_bitcast_fusion
  3.6 1.7 collective-permute-start
  5.4 2.9 %collective-permute-start.1 = (bf16[1,3,32,1024]{3,0,2,1:T(2,128)(2,1)S(1)}, bf16[1,3,32,1024]{3,0,2,1:T(2,128)(2,1)S(1)}, u32[]{:S(2)}, u32[]{:S(2)}) collective-permute-start(bf16[1,3,32,1024]{3,0,2,1:T(2,128)(2,1)S(1)} %get-tuple-element.6), channel_id=1, source_target_pairs={{0,64},{32,96},{64,0},{96,32},{1,65},{33,97},{65,1},{97,33},{2,66}... | collective-permute-start | bytes 589832 | tf_op jit(solution)/shard_map/ppermute | solution.py:25
  8.3 1.3 collective-permute-start.2
  9.6 0.1 copy.46
  9.7 0.1 reshape.67
  9.9 6.0 %collective-permute-done = bf16[1,3,32,1024]{3,0,2,1:T(2,128)(2,1)S(1)} collective-permute-done((bf16[1,3,32,1024]{3,0,2,1:T(2,128)(2,1)S(1)}, bf16[1,3,32,1024]{3,0,2,1:T(2,128)(2,1)S(1)}, u32[]{:S(2)}, u32[]{:S(2)}) %collective-permute-start) | collective-permute-done | bytes 196640 | tf_op jit(solution)/shard_map/ppermute | solution.py:25
  15.9 2.6 %dynamic_update_slice.9 = bf16[4,3,32,1024]{3,0,2,1:T(4,128)(2,1)S(1)} dynamic-update-slice(bf16[4,3,32,1024]{3,0,2,1:T(4,128)(2,1)S(1)} %bitcast.50, bf16[1,3,32,1024]{3,0,2,1:T(2,128)(2,1)S(1)} %collective-permute-done, s32[]{:T(128)S(6)} %select_n.62, s32[]{:T(128)} %constant.57.clone.1, s32[]{:T(128)} %constant.57.clone.1, s32[]{:T(128)} %constant.57.clone.1) | dynamic-update-slice | bytes 393220 | tf_op jit(solution)/shard_map/dynamic_update_slice | solution.py:26
  18.6 7.0 %collective-permute-done.1 = bf16[1,3,32,1024]{3,0,2,1:T(2,128)(2,1)S(1)} collective-permute-done((bf16[1,3,32,1024]{3,0,2,1:T(2,128)(2,1)S(1)}, bf16[1,3,32,1024]{3,0,2,1:T(2,128)(2,1)S(1)}, u32[]{:S(2)}, u32[]{:S(2)}) %collective-permute-start.1) | collective-permute-done | bytes 196640 | tf_op jit(solution)/shard_map/ppermute | solution.py:25
  25.5 2.6 %dynamic_update_slice.10 = bf16[4,3,32,1024]{3,0,2,1:T(4,128)(2,1)S(1)} dynamic-update-slice(bf16[4,3,32,1024]{3,0,2,1:T(4,128)(2,1)S(1)} %dynamic_update_slice.9, bf16[1,3,32,1024]{3,0,2,1:T(2,128)(2,1)S(1)} %collective-permute-done.1, s32[]{:T(128)S(6)} %select_n.66, s32[]{:T(128)} %constant.57.clone.1, s32[]{:T(128)} %constant.57.clone.1, s32[]{:T(128)} %constant.57.clone.1) | dynamic-update-slice | bytes 393220 | tf_op jit(solution)/shard_map/dynamic_update_slice | solution.py:26
  28.2 2.7 %dynamic_update_slice.11 = bf16[4,3,32,1024]{3,0,2,1:T(4,128)(2,1)S(1)} dynamic-update-slice(bf16[4,3,32,1024]{3,0,2,1:T(4,128)(2,1)S(1)} %dynamic_update_slice.10, bf16[1,3,32,1024]{3,0,2,1:T(2,128)(2,1)S(1)} %collective-permute-done.2, s32[]{:T(128)S(6)} %select_n.70, s32[]{:T(128)} %constant.57.clone.1, s32[]{:T(128)} %constant.57.clone.1, s32[]{:T(128)} %constant.57.clone.1) | dynamic-update-slice | bytes 393220 | tf_op jit(solution)/shard_map/dynamic_update_slice | solution.py:26
  30.8 0.2 copy.44
  31.1 0.4 copy.45
  31.4 0.0 copy-start.3
  31.5 5.0 %gather_fusion = bf16[1024,384]{1,0:T(8,128)(2,1)} fusion(bf16[1024,384]{1,0:T(8,128)(2,1)S(1)} %bitcast.48, s32[1024]{0:T(1024)S(1)} %broadcast_clamp_fusion), kind=kCustom, calls=%fused_computation | custom fusion | bytes 1576960 | tf_op jit(solution)/shard_map/gather | solution.py:86
  36.5 11.5 %all-to-all-start = ((bf16[128,8,384]{2,1,0:T(8,128)(2,1)}), bf16[128,8,384]{2,1,0:T(8,128)(2,1)S(1)}, u32[]{:S(2)}, u32[]{:S(2)}) async-start(bf16[128,8,384]{2,1,0:T(8,128)(2,1)} %bitcast.9), calls=%async_computation | async-start | bytes 1572864 | tf_op jit(solution)/shard_map/all_to_all | solution.py:31
  47.9 20.8 %convert_subtract_fusion = f32[616,8192]{1,0:T(8,128)} fusion(bf16[616,8192]{1,0:T(8,128)(2,1)} %param.11, f32[616,8]{0,1:T(8,128)S(1)} %copy-done.3, f32[8,8192]{1,0:T(8,128)S(1)} %copy-done), kind=kOutput, calls=%fused_computation.7 | convolution fusion | flops 494534656 | bytes 30559488 | tf_op jit(solution)/shard_map/dot_general | solution.py:50
  68.7 33.1 %gather_fusion.1 = bf16[8192,384]{1,0:T(8,128)(2,1)} fusion(bf16[1024,384]{1,0:T(8,128)(2,1)S(1)} %bitcast.47, s32[8192]{0:T(1024)S(1)} %fusion.12), kind=kCustom, calls=%fused_computation.1 | custom fusion | bytes 12615680 | tf_op jit(solution)/shard_map/gather | solution.py:88
  101.8 24.5 %fusion.2 = f32[8,1024,384]{2,1,0:T(8,128)} fusion(bf16[8,616,384]{2,1,0:T(8,128)(2,1)} %param.10, f32[77,8,8,1024]{3,2,1,0:T(8,128)} %bitcast.49, f32[616,8]{0,1:T(8,128)S(1)} %multiply_bitcast_fusion, bf16[8,1024,384]{2,1,0:T(8,128)(2,1)} %bitcast.52), kind=kOutput, calls=%fused_computation.8 | convolution fusion | flops 7766212608 | bytes 42863872 | tf_op jit(solution)/shard_map/tcf,cto->tof/dot_general | solution.py:59
  126.3 50.4 %scatter_custom_fusion = f32[1024,384]{1,0:T(8,128)} fusion(s32[8192]{0:T(1024)S(1)} %copy-done.2, f32[8192,384]{1,0:T(8,128)} %bitcast.57, f32[]{:T(128)} %constant.55.clone.1), kind=kCustom, calls=%fused_computation.14 | custom fusion | flops 3145728 | bytes 1573376 | tf_op jit(solution)/shard_map/scatter-add | solution.py:90
  176.8 9.6 %all-to-all-start.1 = ((f32[128,8,384]{2,1,0:T(8,128)}), f32[128,8,384]{2,1,0:T(8,128)S(1)}, u32[]{:S(2)}, u32[]{:S(2)}) async-start(f32[128,8,384]{2,1,0:T(8,128)} %bitcast.14), calls=%async_computation.1 | async-start | bytes 3145728 | tf_op jit(solution)/shard_map/all_to_all | solution.py:35
  186.4 0.1 copy.40
  186.5 0.1 reshape.91
  186.6 24.7 %all-to-all-done.1 = f32[128,8,384]{2,1,0:T(8,128)S(1)} async-done(((f32[128,8,384]{2,1,0:T(8,128)}), f32[128,8,384]{2,1,0:T(8,128)S(1)}, u32[]{:S(2)}, u32[]{:S(2)}) %all-to-all-start.1) | async-done | bytes 1572896 | tf_op jit(solution)/shard_map/all_to_all | solution.py:35
  211.2 7.1 %scatter_custom_fusion.1 = f32[1024,384]{1,0:T(8,128)S(1)} fusion(s32[1024]{0:T(1024)S(1)} %reshape.91, f32[128,8,384]{2,1,0:T(8,128)S(1)} %all-to-all-done.1, f32[]{:T(128)} %constant.55.clone.1), kind=kCustom, calls=%fused_computation.11 | custom fusion | flops 393216 | bytes 3145732 | tf_op jit(solution)/shard_map/scatter-add | solution.py:92
  218.3 0.5 copy.48
  218.8 1.1 copy.49
  219.9 0.0 copy-start.1
  219.9 28.6 %all_to_all.28 = f32[3,128,1024]{2,0,1:T(4,128)S(1)} all-to-all(f32[3,128,1024]{2,0,1:T(4,128)S(1)} %copy.49), channel_id=1, replica_groups=mesh['lev'=4,'col'=32] {'lev'}, dimensions={1} | all-to-all | bytes 3145728 | tf_op jit(solution)/shard_map/all_to_all | solution.py:98
  248.5 0.9 copy.50
  249.4 1.3 copy.53
  (19 shorter events, 0.1 us)
Async XLA Ops:
  0.0 47.9 %copy-start = (f32[8,8192]{1,0:T(8,128)S(1)}, f32[8,8192]{1,0:T(8,128)}, u32[]{:S(2)}) copy-start(f32[8,8192]{1,0:T(8,128)} %param.12) | copy-start | bytes 786436
  0.0 9.6 %copy-start.5 = (s32[1,128,8]{1,2,0:T(8,128)S(1)}, s32[1,128,8]{1,2,0:T(8,128)}, u32[]{:S(2)}) copy-start(s32[1,128,8]{1,2,0:T(8,128)} %param.16) | copy-start | bytes 12292
  0.0 9.8 %copy-start.2 = (s32[8192]{0:T(1024)S(1)}, s32[8192]{0:T(1024)}, u32[]{:S(2)}) copy-start(s32[8192]{0:T(1024)} %param.17) | copy-start | bytes 98308
  0.0 9.9 %copy-start.6 = (f32[616]{0:T(1024)S(1)}, f32[616]{0:T(1024)}, u32[]{:S(2)}) copy-start(f32[616]{0:T(1024)} %param.14) | copy-start | bytes 7396
  0.0 9.9 %copy-start.4 = (s32[8,616]{1,0:T(8,128)S(1)}, s32[8,616]{1,0:T(8,128)}, u32[]{:S(2)}) copy-start(s32[8,616]{1,0:T(8,128)} %param.15) | copy-start | bytes 59140
  3.6 12.3 %collective-permute-start = (bf16[1,3,32,1024]{3,0,2,1:T(2,128)(2,1)S(1)}, bf16[1,3,32,1024]{3,0,2,1:T(2,128)(2,1)S(1)}, u32[]{:S(2)}, u32[]{:S(2)}) collective-permute-start(bf16[1,3,32,1024]{3,0,2,1:T(2,128)(2,1)S(1)} %get-tuple-element.7), channel_id=1, source_target_pairs={{0,32},{32,64},{64,96},{96,0},{1,33},{33,65},{65,97},{97,1},{2,34}... | collective-permute-start | bytes 589832 | tf_op jit(solution)/shard_map/ppermute | solution.py:25
  5.4 20.2 %collective-permute-start.1 = (bf16[1,3,32,1024]{3,0,2,1:T(2,128)(2,1)S(1)}, bf16[1,3,32,1024]{3,0,2,1:T(2,128)(2,1)S(1)}, u32[]{:S(2)}, u32[]{:S(2)}) collective-permute-start(bf16[1,3,32,1024]{3,0,2,1:T(2,128)(2,1)S(1)} %get-tuple-element.6), channel_id=1, source_target_pairs={{0,64},{32,96},{64,0},{96,32},{1,65},{33,97},{65,1},{97,33},{2,66}... | collective-permute-start | bytes 589832 | tf_op jit(solution)/shard_map/ppermute | solution.py:25
  8.3 19.9 %collective-permute-start.2 = (bf16[1,3,32,1024]{3,0,2,1:T(2,128)(2,1)S(1)}, bf16[1,3,32,1024]{3,0,2,1:T(2,128)(2,1)S(1)}, u32[]{:S(2)}, u32[]{:S(2)}) collective-permute-start(bf16[1,3,32,1024]{3,0,2,1:T(2,128)(2,1)S(1)} %get-tuple-element.5), channel_id=1, source_target_pairs={{0,96},{32,0},{64,32},{96,64},{1,97},{33,1},{65,33},{97,65},{2,98}... | collective-permute-start | bytes 589832 | tf_op jit(solution)/shard_map/ppermute | solution.py:25
  31.4 16.5 %copy-start.3 = (f32[616,8]{0,1:T(8,128)S(1)}, f32[616,8]{0,1:T(8,128)}, u32[]{:S(2)}) copy-start(f32[616,8]{0,1:T(8,128)} %param.13) | copy-start | bytes 59140
  36.5 32.3 %all-to-all-start = ((bf16[128,8,384]{2,1,0:T(8,128)(2,1)}), bf16[128,8,384]{2,1,0:T(8,128)(2,1)S(1)}, u32[]{:S(2)}, u32[]{:S(2)}) async-start(bf16[128,8,384]{2,1,0:T(8,128)(2,1)} %bitcast.9), calls=%async_computation | async-start | bytes 1572864 | tf_op jit(solution)/shard_map/all_to_all | solution.py:31
  176.8 34.5 %all-to-all-start.1 = ((f32[128,8,384]{2,1,0:T(8,128)}), f32[128,8,384]{2,1,0:T(8,128)S(1)}, u32[]{:S(2)}, u32[]{:S(2)}) async-start(f32[128,8,384]{2,1,0:T(8,128)} %bitcast.14), calls=%async_computation.1 | async-start | bytes 3145728 | tf_op jit(solution)/shard_map/all_to_all | solution.py:35
  219.9 30.9 %copy-start.1 = (f32[8,8192]{1,0:T(8,128)S(1)}, f32[8,8192]{1,0:T(8,128)}, u32[]{:S(2)}) copy-start(f32[8,8192]{1,0:T(8,128)} %param.12) | copy-start | bytes 786436
